TPU v7x, 32 devices: a whole 2x2x4 slice. The times are simulated.
32 devices in a mesh: dp: 8 (over z, core), pos: 4 (over y, x).
Axes of the slice: x: 2, y: 2, z: 4, core: 2. Of those that a mesh axis runs over, the one named last changes fastest.
Arguments:
- features: bfloat16 [64, 128, 224], P(('dp', 'pos')), may hold values from -6 to 6
- counts: int32 [32], P(('dp', 'pos')), may hold values from 1 to 2, as said below
- channel_order: int32 [224], replicated, may hold values from 0 to 223, each once
Outputs:
- mean: float32 [128, 100], P('pos')
- covariance: float32 [128, 100, 100], P('pos')
Inputs may be any that keep to these rules, and one draw needn't show every extreme that they name: `counts`: some device has all 2 slots live and some device only one.
All inputs are finite; a program needn't handle non-finite values.
Results may differ from a plain program's by a relative error of at most 0.0003.
Values may be sent and summed in bfloat16 or wider, within the bound.
No kernel may reach another device: no remote copies, remote signals or barrier semaphores. Data moves between devices by JAX's collectives and lax.ppermute only.
A program may use at most 128 MiB of HBM per device.

v0:
```python
import jax
import jax.numpy as jnp
from jax import lax
from jax.sharding import PartitionSpec as P

CH = 100


def local_stats(received, source_counts, slots, rows, width):
    sources = source_counts.shape[0]
    samples = received.reshape(sources * slots, rows, width).astype(jnp.float32)
    live_mask = (jnp.arange(slots, dtype=jnp.float32)[None, :] < source_counts[:, None]).astype(
        jnp.float32
    )
    live_mask = live_mask.reshape(sources * slots)
    group_count = jnp.sum(source_counts).reshape(1)
    group_sums = jnp.sum(samples, axis=0)
    group_mean = group_sums / group_count
    centered = (samples - group_mean[None]) * live_mask[:, None, None]
    products = jnp.einsum("gpc,gpd->pcd", centered, centered, precision=lax.Precision.HIGHEST)
    return (group_count, group_sums, group_mean, products)


def common_mean(group_count, group_sums, group_mean):
    total_count, total_sums = lax.psum((group_count, group_sums), "dp")
    mean = total_sums / total_count
    offset = group_mean - mean
    weighted = offset * group_count
    return (total_count, mean, offset, weighted)


def on_device(features, counts, channel_order):
    slots, positions, channels = features.shape
    groups = lax.axis_size("pos")
    pos_dev = positions // groups
    kept = channel_order[:CH]
    picker = (kept[None, :] == jnp.arange(channels, dtype=jnp.int32)[:, None]).astype(jnp.bfloat16)
    owned = counts[0]
    slot_live = (jnp.arange(slots, dtype=jnp.int32) < owned).astype(jnp.bfloat16)
    embed = jnp.dot(
        features.reshape(slots * positions, channels), picker, preferred_element_type=jnp.float32
    )
    embed = embed.astype(jnp.bfloat16).reshape(slots, positions, CH) * slot_live[:, None, None]
    identity = jnp.eye(CH, dtype=jnp.float32)
    packed = embed.reshape(slots, groups, pos_dev * CH)
    owned_wire = jnp.broadcast_to(owned.astype(jnp.bfloat16).reshape(1, 1, 1), (1, groups, 1))
    received, source_counts = (
        lax.all_to_all(packed, "pos", split_axis=1, concat_axis=0, tiled=True),
        lax.all_to_all(owned_wire, "pos", split_axis=1, concat_axis=0, tiled=True),
    )
    source_counts = source_counts.reshape(groups).astype(jnp.float32)
    group_count, group_sums, group_mean, products = local_stats(
        received, source_counts, slots, pos_dev, CH
    )
    total_count, mean, offset, weighted = common_mean(group_count, group_sums, group_mean)
    own_term = products + offset[:, :, None] * weighted[:, None, :]
    summed = lax.psum(own_term, "dp")
    covariance = summed / (total_count[0] - 1.0) + 0.01 * identity
    return (mean, covariance)


def solution(mesh):
    in_specs = (P(("dp", "pos"), None, None), P(("dp", "pos")), P())
    out_specs = (P("pos", None), P("pos", None, None))
    return jax.shard_map(
        on_device, mesh=mesh, in_specs=in_specs, out_specs=out_specs, check_vma=False
    )
```

profile of v0, /device:TPU:0, one launch (start us, length us, event | category | flops | bytes accessed | tf_op | source)
XLA Modules:
  0.0 129.7 jit_solution(13337276662901932767)
XLA Ops:
  7.2 0.0 copy-start
  7.9 0.6 broadcast_in_dim.2
  8.4 5.2 %all-to-all-start.1 = ((bf16[1,4,1]{2,0,1:T(2,128)(2,1)}), bf16[1,4,1]{2,0,1:T(2,128)(2,1)S(1)}, u32[]{:S(2)}, u32[]{:S(2)}) async-start(bf16[1,4,1]{2,0,1:T(2,128)(2,1)} %broadcast_in_dim.2), calls=%async_computation.1 | async-start | bytes 4096 | tf_op jit(solution)/shard_map/all_to_all | solution.py:49
  13.6 0.7 slice.3
  14.3 0.0 copy-done
  14.3 0.2 fusion
  14.5 0.1 copy.19
  14.6 0.2 reshape.81
  14.8 0.1 broadcast_multiply_fusion
  14.9 0.7 copy.20
  15.6 2.6 %all-to-all-done.1 = bf16[1,4,1]{2,0,1:T(2,128)(2,1)S(1)} async-done(((bf16[1,4,1]{2,0,1:T(2,128)(2,1)}), bf16[1,4,1]{2,0,1:T(2,128)(2,1)S(1)}, u32[]{:S(2)}, u32[]{:S(2)}) %all-to-all-start.1) | async-done | bytes 40 | tf_op jit(solution)/shard_map/all_to_all | solution.py:49
  18.2 3.3 %all-to-all-start = ((bf16[2,4,3200]{2,0,1:T(2,128)(2,1)}), bf16[2,4,3200]{2,0,1:T(2,128)(2,1)S(1)}, u32[]{:S(2)}, u32[]{:S(2)}) async-start(bf16[2,4,3200]{2,0,1:T(2,128)(2,1)} %copy.20), calls=%async_computation | async-start | bytes 102400 | tf_op jit(solution)/shard_map/all_to_all | solution.py:48
  21.5 0.0 all-reduce.3.cloned.1.call-start
  21.5 0.7 convert_reduce_fusion.1
  22.2 0.1 fusion.6
  22.3 0.1 reshape.85
  22.4 3.9 %all-to-all-done = bf16[2,4,3200]{2,0,1:T(2,128)(2,1)S(1)} async-done(((bf16[2,4,3200]{2,0,1:T(2,128)(2,1)}), bf16[2,4,3200]{2,0,1:T(2,128)(2,1)S(1)}, u32[]{:S(2)}, u32[]{:S(2)}) %all-to-all-start) | async-done | bytes 51232 | tf_op jit(solution)/shard_map/all_to_all | solution.py:48
  26.2 0.1 convert_reduce_fusion
  26.3 0.1 reduce_sum.21
  26.5 0.3 reshape.84
  26.7 27.4 %all-reduce = (f32[32,100]{1,0:T(8,128)S(1)}, f32[]{:T(128)}) all-reduce(f32[32,100]{1,0:T(8,128)S(1)} %reduce_sum.21, f32[]{:T(128)} %get-tuple-element.11), channel_id=1, replica_groups=mesh['dp'=8,'pos'=4] {'dp'}, use_global_device_ids=true, to_apply=%region_1.0 | all-reduce | flops 3201 | bytes 25608 | tf_op jit(solution)/shard_map/psum | solution.py:25
  54.2 1.9 %broadcast_multiply_fusion.1 = (f32[32,100]{1,0:T(8,128)S(1)}, f32[32,100]{1,0:T(8,128)S(1)}, f32[32,100]{1,0:T(8,128)S(1)}, f32[32,100]{1,0:T(8,128)}) fusion(f32[]{:T(128)} %get-tuple-element.11, f32[32,100]{1,0:T(8,128)S(1)} %reduce_sum.21, f32[32,100]{1,0:T(8,128)S(1)} %get-tuple-element.12, f32[]{:T(128)} %get-tuple-element.13), kind=kLoop, calls=%fused_computation.15 | loop fusion | flops 12800 | bytes 76808 | tf_op jit(solution)/shard_map/mul | solution.py:28
  56.1 0.1 subtract_multiply_fusion
  56.2 4.4 %multiply_add_fusion = f32[32,100,100]{2,1,0:T(8,128)} fusion(f32[32,100]{1,0:T(8,128)S(1)} %get-tuple-element.14, f32[32,100]{1,0:T(8,128)S(1)} %get-tuple-element.15, f32[8,32,100]{2,1,0:T(8,128)S(1)} %subtract_multiply_fusion), kind=kOutput, calls=%fused_computation.1 | convolution fusion | flops 31360000 | bytes 1408000 | tf_op jit(solution)/shard_map/gpc,gpd->pcd/dot_general | solution.py:20
  60.6 0.0 all-reduce.3.cloned.1.call-update
  61.3 58.5 %all-reduce.3.cloned.1.call-done = f32[32,100,100]{2,1,0:T(8,128)} async-done(((f32[32,100,100]{2,1,0:T(8,128)}), f32[32,100,100]{2,1,0:T(8,128)}) %all-reduce.3.cloned.1.call-update) | async-done | bytes 1280016 | tf_op jit(solution)/shard_map/psum | solution.py:57
  119.8 1.6 %divide_add_fusion = f32[32,100,100]{2,1,0:T(8,128)S(1)} fusion(f32[32,100,100]{2,1,0:T(8,128)} %all-reduce.3.cloned.1.call-done, f32[100,100]{1,0:T(8,128)S(1)} %fusion.5, f32[]{:T(128)S(6)} %sub.17), kind=kLoop, calls=%fused_computation | loop fusion | flops 640000 | bytes 2600004 | tf_op jit(solution)/shard_map/add | solution.py:58
  121.4 1.5 %copy.23 = f32[32,100,100]{2,0,1:T(8,128)} copy(f32[32,100,100]{2,1,0:T(8,128)S(1)} %divide_add_fusion) | data formatting | bytes 2560000
  (3 shorter events, 0.1 us)
Async XLA Ops:
  7.2 7.1 %copy-start = (bf16[2,128,224]{1,2,0:T(8,128)(2,1)S(1)}, bf16[2,128,224]{1,2,0:T(8,128)(2,1)}, u32[]{:S(2)}) copy-start(bf16[2,128,224]{1,2,0:T(8,128)(2,1)} %param.3) | copy-start | bytes 344068
  8.4 9.7 %all-to-all-start.1 = ((bf16[1,4,1]{2,0,1:T(2,128)(2,1)}), bf16[1,4,1]{2,0,1:T(2,128)(2,1)S(1)}, u32[]{:S(2)}, u32[]{:S(2)}) async-start(bf16[1,4,1]{2,0,1:T(2,128)(2,1)} %broadcast_in_dim.2), calls=%async_computation.1 | async-start | bytes 4096 | tf_op jit(solution)/shard_map/all_to_all | solution.py:49
  18.2 8.1 %all-to-all-start = ((bf16[2,4,3200]{2,0,1:T(2,128)(2,1)}), bf16[2,4,3200]{2,0,1:T(2,128)(2,1)S(1)}, u32[]{:S(2)}, u32[]{:S(2)}) async-start(bf16[2,4,3200]{2,0,1:T(2,128)(2,1)} %copy.20), calls=%async_computation | async-start | bytes 102400 | tf_op jit(solution)/shard_map/all_to_all | solution.py:48
  21.5 98.3 %all-reduce.3.cloned.1.call-start = ((), (), s32[]{:S(2)}) async-start(), calls=%async_computation.2 | async-start | bytes 3407872 | tf_op jit(solution)/shard_map/psum | solution.py:57
Sparse Core Ops, SparseCore 0:
  60.7 59.0 all-reduce.2
where the time goes:
time: 130 us
  waiting for transfers between devices  65 us (50%)
  blocking collectives  27.4 us (21%)
  between operations  15.4 us (12%)
  starting transfers between devices  8.48 us (7%)
  other arithmetic  4.59 us (4%)
  matrix products  4.57 us (4%)
  local copies, waits for them, and re-layouts  4.13 us (3%)
    psum x1, waiting for transfers between devices, on_device(): summed = lax.psum(own_term, 'dp')  58.5 us
    psum x1, blocking collectives, common_mean(): total_count, total_sums = lax.psum((group_count, group_sums), 'dp')  27.4 us
    all_to_all x1, starting transfers between devices, on_device(): lax.all_to_all(owned_wire, 'pos', split_axis=1, concat_axis=0, tiled=True)  5.16 us
    dot_general x1, matrix products, local_stats(): jnp.einsum('gpc,gpd->pcd', centered, centered, precision=lax.Precision.HI...  4.36 us
    all_to_all x1, waiting for transfers between devices, on_device(): lax.all_to_all(packed, 'pos', split_axis=1, concat_axis=0, tiled=True)  3.88 us
    all_to_all x1, starting transfers between devices, on_device(): lax.all_to_all(packed, 'pos', split_axis=1, concat_axis=0, tiled=True)  3.28 us
    all_to_all x1, waiting for transfers between devices, on_device(): lax.all_to_all(owned_wire, 'pos', split_axis=1, concat_axis=0, tiled=True)  2.61 us
  transfers between devices with their start and end apart: 3, of which 3 were waited for; matrix products, arithmetic and copies ran while one was open for 2% of the time, Pallas kernels for 0%

commit v1 on v0

--- a/solution.py
+++ b/solution.py
@@ -54,7 +54,9 @@
     )
     total_count, mean, offset, weighted = common_mean(group_count, group_sums, group_mean)
     own_term = products + offset[:, :, None] * weighted[:, None, :]
-    summed = lax.psum(own_term, "dp")
+    summed = own_term
+    for hop in (1, 2, 4):
+        summed = summed + lax.ppermute(summed, "dp", [(dev, dev ^ hop) for dev in range(8)])
     covariance = summed / (total_count[0] - 1.0) + 0.01 * identity
     return (mean, covariance)
 

time: 130 us -> 174 us (1.34)
  waiting for transfers between devices: 65 us -> 121 us
  between operations: 15.4 us -> 2 us
  local copies, waits for them, and re-layouts: 4.13 us -> 6.23 us
    ppermute x0 -> x3, waiting for transfers between devices: none -> 114 us  [on_device(): lax.ppermute(summed, 'dp', [(dev, dev ^ hop) for dev in range(8)])]
    psum x1 -> x0, waiting for transfers between devices: 58.5 us -> none  [on_device(): summed = lax.psum(own_term, 'dp')]
    add x0 -> x3, local copies, waits for them, and re-layouts: none -> 2.1 us  [the longest x2 1.78 us: on_device(): summed + lax.ppermute(summed, 'dp', [(dev, dev ^ hop) for dev in range(8)])]
    add x0 -> x2, other arithmetic: none -> 1.94 us  [on_device(): summed + lax.ppermute(summed, 'dp', [(dev, dev ^ hop) for dev in range(8)])]
  transfers between devices with their start and end apart: 3 -> 5, of which waited for: 3 -> 5; matrix products, arithmetic and copies ran while one was open for 2% -> 2% of each run, Pallas kernels for 0% -> 0%
where the time goes in v1:
time: 174 us
  waiting for transfers between devices  121 us (70%)
  blocking collectives  27.4 us (16%)
  starting transfers between devices  8.58 us (5%)
  local copies, waits for them, and re-layouts  6.23 us (4%)
  other arithmetic  5.82 us (3%)
  matrix products  3.42 us (2%)
  between operations  2 us (1%)
    ppermute x3, waiting for transfers between devices, on_device(): lax.ppermute(summed, 'dp', [(dev, dev ^ hop) for dev in range(8)])  114 us
    psum x1, blocking collectives, common_mean(): total_count, total_sums = lax.psum((group_count, group_sums), 'dp')  27.4 us
    all_to_all x1, starting transfers between devices, on_device(): lax.all_to_all(owned_wire, 'pos', split_axis=1, concat_axis=0, tiled=True)  5.16 us
    all_to_all x1, waiting for transfers between devices, on_device(): lax.all_to_all(packed, 'pos', split_axis=1, concat_axis=0, tiled=True)  3.93 us
  transfers between devices with their start and end apart: 5, of which 5 were waited for; matrix products, arithmetic and copies ran while one was open for 2% of the time, Pallas kernels for 0%

profile of v1, /device:TPU:0, one launch (start us, length us, event | category | flops | bytes accessed | tf_op | source)
XLA Modules:
  0.0 174.0 jit_solution(13614635243206103722)
XLA Ops:
  0.6 0.0 copy-start
  1.3 0.6 broadcast_in_dim.2
  1.9 5.2 %all-to-all-start.1 = ((bf16[1,4,1]{2,0,1:T(2,128)(2,1)}), bf16[1,4,1]{2,0,1:T(2,128)(2,1)S(1)}, u32[]{:S(2)}, u32[]{:S(2)}) async-start(bf16[1,4,1]{2,0,1:T(2,128)(2,1)} %broadcast_in_dim.2), calls=%async_computation.1 | async-start | bytes 4096 | tf_op jit(solution)/shard_map/all_to_all | solution.py:49
  7.1 0.7 slice.3
  7.8 0.0 copy-done
  7.8 0.2 fusion.2
  8.0 0.1 copy.25
  8.1 0.2 reshape.81
  8.3 0.1 broadcast_multiply_fusion
  8.4 0.7 copy.26
  9.0 2.6 %all-to-all-done.1 = bf16[1,4,1]{2,0,1:T(2,128)(2,1)S(1)} async-done(((bf16[1,4,1]{2,0,1:T(2,128)(2,1)}), bf16[1,4,1]{2,0,1:T(2,128)(2,1)S(1)}, u32[]{:S(2)}, u32[]{:S(2)}) %all-to-all-start.1) | async-done | bytes 40 | tf_op jit(solution)/shard_map/all_to_all | solution.py:49
  11.6 3.3 %all-to-all-start = ((bf16[2,4,3200]{2,0,1:T(2,128)(2,1)}), bf16[2,4,3200]{2,0,1:T(2,128)(2,1)S(1)}, u32[]{:S(2)}, u32[]{:S(2)}) async-start(bf16[2,4,3200]{2,0,1:T(2,128)(2,1)} %copy.26), calls=%async_computation | async-start | bytes 102400 | tf_op jit(solution)/shard_map/all_to_all | solution.py:48
  14.9 0.7 convert_reduce_fusion.1
  15.6 0.1 fusion.8
  15.7 0.1 reshape.85
  15.8 3.9 %all-to-all-done = bf16[2,4,3200]{2,0,1:T(2,128)(2,1)S(1)} async-done(((bf16[2,4,3200]{2,0,1:T(2,128)(2,1)}), bf16[2,4,3200]{2,0,1:T(2,128)(2,1)S(1)}, u32[]{:S(2)}, u32[]{:S(2)}) %all-to-all-start) | async-done | bytes 51232 | tf_op jit(solution)/shard_map/all_to_all | solution.py:48
  19.7 0.1 convert_reduce_fusion
  19.8 0.1 reduce_sum.21
  19.9 0.3 reshape.84
  20.2 27.4 %all-reduce = (f32[32,100]{1,0:T(8,128)S(1)}, f32[]{:T(128)}) all-reduce(f32[32,100]{1,0:T(8,128)S(1)} %reduce_sum.21, f32[]{:T(128)} %get-tuple-element.11), channel_id=1, replica_groups=mesh['dp'=8,'pos'=4] {'dp'}, use_global_device_ids=true, to_apply=%region_1.0 | all-reduce | flops 3201 | bytes 25608 | tf_op jit(solution)/shard_map/psum | solution.py:25
  47.6 1.9 %broadcast_multiply_fusion.1 = (f32[32,100]{1,0:T(8,128)S(1)}, f32[32,100]{1,0:T(8,128)S(1)}, f32[32,100]{1,0:T(8,128)S(1)}, f32[32,100]{1,0:T(8,128)}) fusion(f32[]{:T(128)} %get-tuple-element.11, f32[32,100]{1,0:T(8,128)S(1)} %reduce_sum.21, f32[32,100]{1,0:T(8,128)S(1)} %get-tuple-element.12, f32[]{:T(128)} %get-tuple-element.13), kind=kLoop, calls=%fused_computation.19 | loop fusion | flops 12800 | bytes 76808 | tf_op jit(solution)/shard_map/mul | solution.py:28
  49.5 0.1 subtract_multiply_fusion
  49.6 3.2 %multiply_add_fusion = f32[32,100,100]{2,1,0:T(8,128)S(1)} fusion(f32[32,100]{1,0:T(8,128)S(1)} %get-tuple-element.14, f32[32,100]{1,0:T(8,128)S(1)} %get-tuple-element.15, f32[8,32,100]{2,1,0:T(8,128)S(1)} %subtract_multiply_fusion), kind=kOutput, calls=%fused_computation.5 | convolution fusion | flops 31360000 | bytes 1408000 | tf_op jit(solution)/shard_map/gpc,gpd->pcd/dot_general | solution.py:20
  52.8 0.3 copy.29
  53.1 0.1 collective-permute-start
  53.2 3.5 %collective-permute-done = f32[32,100,100]{2,0,1:T(8,128)S(1)} collective-permute-done((f32[32,100,100]{2,0,1:T(8,128)S(1)}, f32[32,100,100]{2,0,1:T(8,128)S(1)}, u32[]{:S(2)}, u32[]{:S(2)}) %collective-permute-start) | collective-permute-done | bytes 1280032 | tf_op jit(solution)/shard_map/ppermute | solution.py:59
  56.7 1.0 copy_add_fusion.2
  57.7 0.3 copy.31
  58.0 0.1 collective-permute-start.1
  58.1 37.8 %collective-permute-done.1 = f32[32,100,100]{2,0,1:T(8,128)S(1)} collective-permute-done((f32[32,100,100]{2,0,1:T(8,128)S(1)}, f32[32,100,100]{2,0,1:T(8,128)S(1)}, u32[]{:S(2)}, u32[]{:S(2)}) %collective-permute-start.1) | collective-permute-done | bytes 1280032 | tf_op jit(solution)/shard_map/ppermute | solution.py:59
  95.9 1.0 copy_add_fusion.1
  96.9 1.5 copy.33
  98.3 0.0 collective-permute-start.2
  98.9 72.7 %collective-permute-done.2 = f32[32,100,100]{2,0,1:T(8,128)S(1)} collective-permute-done((f32[32,100,100]{2,0,1:T(8,128)}, f32[32,100,100]{2,0,1:T(8,128)S(1)}, u32[]{:S(2)}, u32[]{:S(2)}) %collective-permute-start.2) | collective-permute-done | bytes 1280032 | tf_op jit(solution)/shard_map/ppermute | solution.py:59
  171.6 1.0 fusion.1
  172.5 1.5 copy.35
  (3 shorter events, 0.1 us)
Async XLA Ops:
  0.6 7.1 %copy-start = (bf16[2,128,224]{1,2,0:T(8,128)(2,1)S(1)}, bf16[2,128,224]{1,2,0:T(8,128)(2,1)}, u32[]{:S(2)}) copy-start(bf16[2,128,224]{1,2,0:T(8,128)(2,1)} %param.3) | copy-start | bytes 344068
  1.9 9.7 %all-to-all-start.1 = ((bf16[1,4,1]{2,0,1:T(2,128)(2,1)}), bf16[1,4,1]{2,0,1:T(2,128)(2,1)S(1)}, u32[]{:S(2)}, u32[]{:S(2)}) async-start(bf16[1,4,1]{2,0,1:T(2,128)(2,1)} %broadcast_in_dim.2), calls=%async_computation.1 | async-start | bytes 4096 | tf_op jit(solution)/shard_map/all_to_all | solution.py:49
  11.6 8.1 %all-to-all-start = ((bf16[2,4,3200]{2,0,1:T(2,128)(2,1)}), bf16[2,4,3200]{2,0,1:T(2,128)(2,1)S(1)}, u32[]{:S(2)}, u32[]{:S(2)}) async-start(bf16[2,4,3200]{2,0,1:T(2,128)(2,1)} %copy.26), calls=%async_computation | async-start | bytes 102400 | tf_op jit(solution)/shard_map/all_to_all | solution.py:48
  53.1 3.6 %collective-permute-start = (f32[32,100,100]{2,0,1:T(8,128)S(1)}, f32[32,100,100]{2,0,1:T(8,128)S(1)}, u32[]{:S(2)}, u32[]{:S(2)}) collective-permute-start(f32[32,100,100]{2,0,1:T(8,128)S(1)} %copy.29), channel_id=1, source_target_pairs={{0,4},{4,0},{8,12},{12,8},{16,20},{20,16},{24,28},{28,24},{1,5},{5... | collective-permute-start | bytes 3840008 | tf_op jit(solution)/shard_map/ppermute | solution.py:59
  58.0 37.9 %collective-permute-start.1 = (f32[32,100,100]{2,0,1:T(8,128)S(1)}, f32[32,100,100]{2,0,1:T(8,128)S(1)}, u32[]{:S(2)}, u32[]{:S(2)}) collective-permute-start(f32[32,100,100]{2,0,1:T(8,128)S(1)} %copy.31), channel_id=1, source_target_pairs={{0,8},{4,12},{8,0},{12,4},{16,24},{20,28},{24,16},{28,20},{1,9},{5... | collective-permute-start | bytes 3840008 | tf_op jit(solution)/shard_map/ppermute | solution.py:59
  98.3 73.2 %collective-permute-start.2 = (f32[32,100,100]{2,0,1:T(8,128)}, f32[32,100,100]{2,0,1:T(8,128)S(1)}, u32[]{:S(2)}, u32[]{:S(2)}) collective-permute-start(f32[32,100,100]{2,0,1:T(8,128)} %copy.33), channel_id=1, source_target_pairs={{0,16},{4,20},{8,24},{12,28},{16,0},{20,4},{24,8},{28,12},{1,17},{... | collective-permute-start | bytes 3840008 | tf_op jit(solution)/shard_map/ppermute | solution.py:59
